TPU v7x, 768 devices: a whole 4x8x12 slice. The times are simulated.
768 devices in a mesh: rep: 96 (over y_hi, z, x), tp: 8 (over y_lo, core).
Axes of the slice: x: 4, y: 8 (y_hi: 2, y_lo: 4; y = y_hi * 4 + y_lo), z: 12, core: 2. Of those that a mesh axis runs over, the one named last changes fastest.
Arguments:
- loader_rows: bfloat16 [24576, 1792], P('rep', 'tp'), may hold values from -14 to 14
- pack_dest: int32 [24576], P('rep'), may hold values from 0 to 24575, as said below
- segment_ids: int32 [96, 256], P('rep'), may hold values from 0 to 11, never falling along the last dimension, each value on 1 to 64 neighbouring positions
- w_qkv: bfloat16 [1792, 3, 1792], P(None, None, 'tp'), may hold values from -0.125 to 0.125
- w_out: bfloat16 [1792, 1792], P('tp'), may hold values from -0.125 to 0.125
- d_out: bfloat16 [24576, 1792], P('rep', 'tp'), may hold values from -6 to 6
Outputs:
- grad_qkv: float32 [5376, 1792], P('rep', 'tp')
- d_packed: bfloat16 [24576, 1792], P('rep', 'tp')
Inputs may be any that keep to these rules, and one draw needn't show every extreme that they name: `pack_dest`: a permutation of all rows; every pack receives at most 3 rows from one loader shard, and exactly 3 from some.
All inputs are finite; a program needn't handle non-finite values.
Results may differ from a plain program's by a relative error of at most 0.034.
The roundings to bfloat16 on the way count: a program that leaves them out, or rounds other values in their place, can miss the bound.
Values may be sent and summed in bfloat16 or wider, within the bound.
A program may use at most 64 MiB of HBM per device.

v0:
```python
import jax
import jax.numpy as jnp
from jax import lax
from jax.sharding import PartitionSpec as P

HEAD_DIM = 112


def attention_grads(rows_full, cot_full, seg_row, w_qkv, w_out):
    tok_count = rows_full.shape[0]
    local_width = w_qkv.shape[2]
    heads_local = local_width // HEAD_DIM
    scale = HEAD_DIM ** (-0.5)
    qkv = jnp.einsum("td,dwc->twc", rows_full, w_qkv, preferred_element_type=jnp.float32).astype(
        jnp.bfloat16
    )
    qkv = qkv.reshape(tok_count, 3, heads_local, HEAD_DIM)
    query, keys, values = (qkv[:, 0], qkv[:, 1], qkv[:, 2])
    scores = jnp.einsum("qhe,khe->hqk", query, keys, preferred_element_type=jnp.float32) * scale
    same = seg_row[:, None] == seg_row[None, :]
    scores = jnp.where(same[None], scores, -jnp.inf)
    expo = jnp.exp(scores - jnp.max(scores, axis=2, keepdims=True))
    probs = expo / jnp.sum(expo, axis=2, keepdims=True)
    probs_b = probs.astype(jnp.bfloat16)
    attn = jnp.einsum("hqk,khe->qhe", probs_b, values, preferred_element_type=jnp.float32).astype(
        jnp.bfloat16
    )
    d_attn = lax.dot_general(
        cot_full, w_out, (((1,), (1,)), ((), ())), preferred_element_type=jnp.float32
    )
    d_attn = d_attn.astype(jnp.bfloat16).reshape(tok_count, heads_local, HEAD_DIM)
    d_prob = jnp.einsum("qhe,khe->hqk", d_attn, values, preferred_element_type=jnp.float32)
    delta = jnp.einsum("qhe,qhe->hq", d_attn, attn, preferred_element_type=jnp.float32)
    d_score = (probs * (d_prob - delta[:, :, None]) * scale).astype(jnp.bfloat16)
    d_query = jnp.einsum("hqk,khe->qhe", d_score, keys, preferred_element_type=jnp.float32).astype(
        jnp.bfloat16
    )
    d_keys = jnp.einsum("hqk,qhe->khe", d_score, query, preferred_element_type=jnp.float32).astype(
        jnp.bfloat16
    )
    d_values = jnp.einsum(
        "hqk,qhe->khe", probs_b, d_attn, preferred_element_type=jnp.float32
    ).astype(jnp.bfloat16)
    return jnp.stack([d_query, d_keys, d_values], axis=1).reshape(tok_count, 3, local_width)


def shards(loader_rows, pack_dest, segment_ids, w_qkv, w_out, d_out):
    tok_count = loader_rows.shape[0]
    width_local = loader_rows.shape[1]
    pack_count = lax.axis_size("rep")
    capacity = -(-tok_count // pack_count)
    target = pack_dest // tok_count
    slot_of = pack_dest % tok_count
    onehot = (target[:, None] == jnp.arange(pack_count, dtype=jnp.int32)[None, :]).astype(jnp.int32)
    rank_in = jnp.sum((jnp.cumsum(onehot, axis=0) - onehot) * onehot, axis=1)
    position = target * capacity + rank_in
    send_rows = (
        jnp.zeros((pack_count * capacity, width_local), jnp.bfloat16).at[position].set(loader_rows)
    )
    send_slots = jnp.full((pack_count * capacity,), tok_count, jnp.int32).at[position].set(slot_of)
    got_rows, got_slots = (
        lax.all_to_all(
            send_rows.reshape(pack_count, capacity, width_local),
            "rep",
            split_axis=0,
            concat_axis=0,
            tiled=True,
        ),
        lax.all_to_all(
            send_slots.reshape(pack_count, capacity), "rep", split_axis=0, concat_axis=0, tiled=True
        ),
    )
    packed = jnp.zeros((tok_count + 1, width_local), jnp.bfloat16)
    packed = packed.at[got_slots.reshape(-1)].set(got_rows.reshape(-1, width_local))[:tok_count]
    rows_full, cot_full = (
        lax.all_gather(packed, "tp", axis=1, tiled=True),
        lax.all_gather(d_out, "tp", axis=1, tiled=True),
    )
    d_qkv = attention_grads(rows_full, cot_full, segment_ids[0], w_qkv, w_out)
    d_partial = jnp.einsum("twc,dwc->td", d_qkv, w_qkv, preferred_element_type=jnp.float32)
    d_packed = lax.psum_scatter(d_partial, "tp", scatter_dimension=1, tiled=True).astype(
        jnp.bfloat16
    )
    full_width = rows_full.shape[1]
    local_width = w_qkv.shape[2]
    norm_factor = (tok_count * pack_count) ** (-0.5)
    partial_grad = jnp.einsum("td,twc->dwc", rows_full, d_qkv, preferred_element_type=jnp.float32)
    partial_grad = partial_grad.reshape(3 * full_width, local_width)
    grad_rows = lax.psum_scatter(partial_grad, "rep", scatter_dimension=0, tiled=True)
    return (grad_rows * norm_factor, d_packed)


def solution(mesh):
    placed = (
        P("rep", "tp"),
        P("rep"),
        P("rep", None),
        P(None, None, "tp"),
        P("tp", None),
        P("rep", "tp"),
    )
    return jax.shard_map(
        shards,
        mesh=mesh,
        in_specs=placed,
        out_specs=(P("rep", "tp"), P("rep", "tp")),
        check_vma=False,
    )
```

profile of v0, /device:TPU:8, one launch (start us, length us, event | category | flops | bytes accessed | tf_op | source)
XLA Modules:
  0.0 844.3 jit_solution(14078944183333293673)
XLA Ops:
  7.2 0.8 and_select_fusion
  8.0 0.6 reduce-window.6
  9.0 1.4 scatter_custom_fusion
  10.5 0.8 all_to_all.9
  11.2 23.6 %all-to-all-start = ((s32[96,1,3]{2,1,0:T(1,128)}), s32[96,1,3]{2,1,0:T(1,128)S(1)}, u32[]{:S(2)}, u32[]{:S(2)}) async-start(s32[96,1,3]{2,1,0:T(1,128)} %bitcast.4), calls=%async_computation | async-start | bytes 98304 | tf_op jit(solution)/shard_map/all_to_all | solution.py:69
  34.8 14.4 %all_gather.7 = bf16[256,1792]{0,1:T(8,128)(2,1)S(1)} all-gather(bf16[256,224]{0,1:T(8,128)(2,1)} %param.11), channel_id=1, replica_groups=mesh['rep'=96,'tp'=8] {'tp'}, dimensions={1}, use_global_device_ids=true | all-gather | bytes 1032192 | tf_op jit(solution)/shard_map/all_gather | solution.py:77
  49.3 1.5 broadcast_compare_fusion
  50.7 1.6 copy.22
  52.4 1.8 scatter_custom_fusion.1
  54.2 0.8 reshape.113
  55.0 0.6 copy-done.3
  55.6 17.9 %all-to-all-start.1 = ((bf16[96,3,224]{2,1,0:T(4,128)(2,1)}), bf16[96,3,224]{2,1,0:T(4,128)(2,1)S(1)}, u32[]{:S(2)}, u32[]{:S(2)}) async-start(bf16[96,3,224]{2,1,0:T(4,128)(2,1)} %reshape.113), calls=%async_computation.1 | async-start | bytes 393216 | tf_op jit(solution)/shard_map/all_to_all | solution.py:62
  73.5 2.2 convolution_convert_fusion
  76.3 1.5 reduce.9
  78.0 15.5 %all-to-all-done.1 = bf16[96,3,224]{2,1,0:T(4,128)(2,1)S(1)} async-done(((bf16[96,3,224]{2,1,0:T(4,128)(2,1)}), bf16[96,3,224]{2,1,0:T(4,128)(2,1)S(1)}, u32[]{:S(2)}, u32[]{:S(2)}) %all-to-all-start.1) | async-done | bytes 129056 | tf_op jit(solution)/shard_map/all_to_all | solution.py:62
  93.6 1.6 scatter_custom_fusion.2
  95.3 16.8 %all_gather.6 = bf16[256,1792]{0,1:T(8,128)(2,1)S(1)} all-gather(bf16[256,224]{0,1:T(8,128)(2,1)S(1)} %copy.42), channel_id=1, replica_groups=mesh['rep'=96,'tp'=8] {'tp'}, dimensions={1}, use_global_device_ids=true | all-gather | bytes 1032192 | tf_op jit(solution)/shard_map/all_gather | solution.py:76
  112.2 0.8 fusion.30
  113.0 0.8 convert_element_type.48
  113.7 2.1 fusion.28
  115.8 1.6 fusion.10
  117.4 2.2 convolution_convert_fusion.1
  119.6 1.4 fusion.6
  121.5 2.4 convolution_bitcast_fusion
  124.0 0.9 pad_maximum_fusion
  124.9 3.0 fusion.29
  128.0 8.4 copy.29
  136.3 9.5 %reshape.117 = f32[5376,224]{1,0:T(8,128)} reshape(f32[1792,3,224]{2,1,0:T(4,128)} %copy.29) | data formatting | bytes 9633792 | tf_op jit(solution)/shard_map/reshape | solution.py:88
  145.8 11.0 %reduce-scatter.5.cloned.1.call-done = f32[256,224]{0,1:T(8,128)} async-done(((f32[256,1792]{0,1:T(8,128)}), f32[256,224]{0,1:T(8,128)}) %reduce-scatter.5.cloned.1.call-update) | async-done | bytes 229392 | tf_op jit(solution)/shard_map/reduce_scatter | solution.py:81
  156.8 1.6 convert_element_type.60
  158.4 677.6 %reduce-scatter.3.cloned.1.call-done = f32[56,224]{1,0:T(8,128)} async-done(((f32[5376,224]{1,0:T(8,128)}), f32[56,224]{1,0:T(8,128)}) %reduce-scatter.3.cloned.1.call-update) | async-done | bytes 50192 | tf_op jit(solution)/shard_map/reduce_scatter | solution.py:89
  836.0 1.4 broadcast_multiply_fusion
  (30 shorter events, 1.9 us)
Async XLA Ops:
  7.2 105.0 %copy-start = (bf16[1792,3,224]{0,2,1:T(8,128)(2,1)S(1)}, bf16[1792,3,224]{0,2,1:T(8,128)(2,1)}, u32[]{:S(2)}) copy-start(bf16[1792,3,224]{0,2,1:T(8,128)(2,1)} %param.9) | copy-start | bytes 7225348
  11.2 43.7 %all-to-all-start = ((s32[96,1,3]{2,1,0:T(1,128)}), s32[96,1,3]{2,1,0:T(1,128)S(1)}, u32[]{:S(2)}, u32[]{:S(2)}) async-start(s32[96,1,3]{2,1,0:T(1,128)} %bitcast.4), calls=%async_computation | async-start | bytes 98304 | tf_op jit(solution)/shard_map/all_to_all | solution.py:69
  55.0 0.6 copy-start.3
  55.6 37.9 %all-to-all-start.1 = ((bf16[96,3,224]{2,1,0:T(4,128)(2,1)}), bf16[96,3,224]{2,1,0:T(4,128)(2,1)S(1)}, u32[]{:S(2)}, u32[]{:S(2)}) async-start(bf16[96,3,224]{2,1,0:T(4,128)(2,1)} %reshape.113), calls=%async_computation.1 | async-start | bytes 393216 | tf_op jit(solution)/shard_map/all_to_all | solution.py:62
  73.5 83.3 %reduce-scatter.5.cloned.1.call-start = ((), (), s32[]{:S(2)}) async-start(), calls=%async_computation.5 | async-start | bytes 2064384 | tf_op jit(solution)/shard_map/reduce_scatter | solution.py:81
  112.2 1.6 copy-start.5
  112.2 3.7 copy-start.4
  119.6 1.4 copy-start.1
  119.6 1.9 copy-start.2
  123.9 712.1 %reduce-scatter.3.cloned.1.call-start = ((), (), s32[]{:S(2)}) async-start(), calls=%async_computation.4 | async-start | bytes 5562368 | tf_op jit(solution)/shard_map/reduce_scatter | solution.py:89
Sparse Core Ops, SparseCore 0:
  124.0 32.7 reduce-scatter.4
  159.9 676.0 reduce-scatter.2
where the time goes:
time: 845 us; the launch traced here: 844 us
  waiting for transfers between devices  704 us (83%)
  starting transfers between devices  41.5 us (5%)
  blocking collectives  31.3 us (4%)
  local copies, waits for them, and re-layouts  27.6 us (3%)
  matrix products  16.1 us (2%)
  between operations  14.2 us (2%)
  other arithmetic  9.44 us (1%)
    reduce_scatter x1, waiting for transfers between devices, shards(): lax.psum_scatter(partial_grad, 'rep', scatter_dimension=0, tiled=True)  678 us
    all_to_all x1, starting transfers between devices, shards(): lax.all_to_all(send_slots.reshape(pack_count, capacity), 'rep', split_axi...  23.6 us
    all_to_all x1, starting transfers between devices, shards(): lax.all_to_all(send_rows.reshape(pack_count, capacity, width_local), 'rep...  17.9 us
  transfers between devices with their start and end apart: 4, of which 3 were waited for; matrix products, arithmetic and copies ran while one was open for 4% of the time, Pallas kernels for 0%

commit v1 on v0

v1 whole, which is shorter than its diff:
```python
import functools

import jax
import jax.numpy as jnp
import numpy as np
from jax import lax
from jax.experimental import pallas as pl
from jax.experimental.pallas import tpu as pltpu
from jax.sharding import PartitionSpec as P

HEAD_DIM = 112
MESH = pl.DeviceIdType.MESH
F32 = jnp.float32
BF16 = jnp.bfloat16


def _dot(a, b, ca, cb):
    return lax.dot_general(a, b, (((ca,), (cb,)), ((), ())), preferred_element_type=F32)


def _nn(a, b):
    return _dot(a, b, 1, 0)


def _nt(a, b):
    return _dot(a, b, 1, 1)


def _tn(a, b):
    return _dot(a, b, 0, 0)


def _onehot(cond):
    return jnp.where(cond, 1.0, 0.0).astype(BF16)


class Sizes:
    def __init__(self, yh, z, x, yl, c, tok, width):
        self.YH, self.Z, self.X, self.YL, self.C = yh, z, x, yl, c
        self.TOK, self.W = tok, width
        self.R, self.T = yh * z * x, yl * c
        self.D = width * self.T
        self.Q = yh * x
        self.CAP = -(-tok // self.R)
        self.B1 = -(-self.Q * self.CAP // 16) * 16
        self.B2 = -(-self.Z * self.CAP // 16) * 16
        self.RPD = 3 * self.D // self.R
        self.RZ = x * self.RPD


def _regroup(s):
    m = np.zeros((s.Q * s.B2, s.Z * s.B1), np.float32)
    for q in range(s.Q):
        for zs in range(s.Z):
            for j in range(s.CAP):
                m[q * s.B2 + zs * s.CAP + j, zs * s.B1 + q * s.CAP + j] = 1.0
    return m


def _kernel(
    s,
    ld, dest, seg, w_hbm, wo_hbm, cot, regroup,
    g_out, d_out,
    wv, wn, wo, s1, r1, s2, r2, xt, ct, dq3, f0, f1, stage, slots, red, xs, xr, acc, yr,
    ps_s, ps_r, pown, py_s, py_r,
    w_sem, z_ss, z_rs, q_ss, q_rs, cg_ss, cg_rs, cf_ss, cf_rs, xg_ss, xg_rs, xf_ss, xf_rs,
    c_ss, c_rs, x_ss, x_rs, y_ss, y_rs, pc_ss, pc_rs, py_ss, py_rs,
):
    W, TOK, Z, X, YH, YL, C, Q = s.W, s.TOK, s.Z, s.X, s.YH, s.YL, s.C, s.Q
    rep, tp = lax.axis_index("rep"), lax.axis_index("tp")
    mx = rep % X
    mz = (rep // X) % Z
    my = rep // (X * Z)
    ml, mc = tp // C, tp % C
    mq = my * X + mx

    def at_z(z):
        return {"rep": (my * Z + z) * X + mx}

    def at_q(q):
        return {"rep": ((q // X) * Z + mz) * X + q % X}

    def at_t(l, c):
        return {"tp": l * C + c}

    def rows(ref, start, size, unit):
        return ref.at[pl.ds(pl.multiple_of(start, unit), size)]

    def send(src, dst, ss, rs, device):
        copy = pltpu.make_async_remote_copy(
            src_ref=src, dst_ref=dst, send_sem=ss, recv_sem=rs, device_id=device, device_id_type=MESH
        )
        copy.start()
        return copy

    partners = [at_z((mz + o) % Z) for o in range(1, Z)]
    partners += [at_q((mq + o) % Q) for o in range(1, Q)]
    partners += [at_t((ml + o) % YL, mc) for o in range(1, YL)]
    partners += [at_t(ml, 1 - mc)]
    barrier = pltpu.get_barrier_semaphore()
    for device in partners:
        pl.semaphore_signal(barrier, inc=1, device_id=device, device_id_type=MESH)

    w_copy = pltpu.make_async_copy(w_hbm, wv, w_sem.at[0])
    w_copy.start()
    wo_copy = pltpu.make_async_copy(wo_hbm, wo, w_sem.at[1])
    wo_copy.start()

    dst = dest[...]
    pack, slot = dst // TOK, dst % TOK
    iota_p = lax.broadcasted_iota(jnp.int32, (128, TOK), 0)
    of_pack = _onehot(iota_p == pack)
    before = _onehot(
        lax.broadcasted_iota(jnp.int32, (TOK, TOK), 0) < lax.broadcasted_iota(jnp.int32, (TOK, TOK), 1)
    )
    rank = jnp.sum(_nn(of_pack, before) * of_pack.astype(F32), axis=0, keepdims=True).astype(jnp.int32)
    px, pz, py = pack % X, (pack // X) % Z, pack // (X * Z)
    place = pz * s.B1 + (py * X + px) * s.CAP + rank
    pick = _onehot(lax.broadcasted_iota(jnp.int32, (Z * s.B1, TOK), 0) == place)
    slot1 = jnp.broadcast_to((slot + 1).astype(F32), (256 - W, TOK)).astype(BF16)
    s1[...] = _nt(pick, jnp.concatenate([ld[...], slot1], axis=0)).astype(BF16)

    pl.semaphore_wait(barrier, len(partners))

    zc = []
    for o in range(1, Z):
        to = (mz + o) % Z
        zc.append(
            send(rows(s1, to * s.B1, s.B1, 16), rows(r1, mz * s.B1, s.B1, 16),
                 z_ss.at[o - 1], z_rs.at[o - 1], at_z(to))
        )
    r1[pl.ds(pl.multiple_of(mz * s.B1, 16), s.B1)] = s1[pl.ds(pl.multiple_of(mz * s.B1, 16), s.B1)]

    def gather(src, buf, ss, rs, fs, fr):
        mine = rows(buf, tp * W, W, 16)
        first = [send(src, mine, ss.at[o - 1], rs.at[o - 1], at_t((ml + o) % YL, mc)) for o in range(1, YL)]
        first.append(send(src, mine, fs.at[0], fr.at[0], at_t(ml, 1 - mc)))

        def rest():
            more = []
            for o in range(1, YL):
                first[o - 1].wait_recv()
                there = rows(buf, ((ml - o + YL) % YL * C + mc) * W, W, 16)
                more.append(send(there, there, fs.at[o], fr.at[o], at_t(ml, 1 - mc)))
            first[-1].wait_recv()
            for copy in more:
                copy.wait_recv()
            return first + more

        return rest

    cot_rest = gather(cot, ct, cg_ss, cg_rs, cf_ss, cf_rs)
    ct[pl.ds(pl.multiple_of(tp * W, 16), W)] = cot[...]

    w_copy.wait()
    for w in range(3):
        for j in range(0, s.D, 128):
            wn[w, pl.ds(j, 128)] = wv[pl.ds(w * W, W), pl.ds(j, 128)].T

    for copy in zc:
        copy.wait_recv()
    s2[...] = _nn(regroup[...], r1[...]).astype(BF16)
    qc = []
    for o in range(1, Q):
        to = (mq + o) % Q
        qc.append(
            send(rows(s2, to * s.B2, s.B2, 16), rows(r2, mq * s.B2, s.B2, 16),
                 q_ss.at[o - 1], q_rs.at[o - 1], at_q(to))
        )
    r2[pl.ds(pl.multiple_of(mq * s.B2, 16), s.B2)] = s2[pl.ds(pl.multiple_of(mq * s.B2, 16), s.B2)]

    sent = cot_rest()
    wo_copy.wait()
    d_attn = _nn(wo[...], ct[...]).astype(BF16)

    for copy in qc:
        copy.wait_recv()
    got = r2[...]
    slots_got = got[:, W:W + 1].astype(F32)
    iota_s = lax.broadcasted_iota(jnp.int32, (Q * s.B2, TOK), 1).astype(F32) + 1.0
    put = _onehot(slots_got == iota_s)
    xt[pl.ds(pl.multiple_of(tp * W, 16), W)] = _tn(got, put)[:W].astype(BF16)
    rows_rest = gather(rows(xt, tp * W, W, 16), xt, xg_ss, xg_rs, xf_ss, xf_rs)
    sent += rows_rest()

    qkv = _nn(wv[...], xt[...]).astype(BF16)
    scale = HEAD_DIM ** (-0.5)
    seg_to = jnp.broadcast_to(seg[...].astype(F32), (TOK, TOK))
    same = seg_to.T == seg_to
    heads = W // HEAD_DIM
    for h in range(heads):
        lo = h * HEAD_DIM
        qt = qkv[lo:lo + HEAD_DIM]
        kt = qkv[W + lo:W + lo + HEAD_DIM]
        vt = qkv[2 * W + lo:2 * W + lo + HEAD_DIM]
        da = d_attn[lo:lo + HEAD_DIM]
        scores = jnp.where(same, _tn(kt, qt) * scale, -jnp.inf)
        expo = jnp.exp(scores - jnp.max(scores, axis=0, keepdims=True))
        probs = expo / jnp.sum(expo, axis=0, keepdims=True)
        probs_b = probs.astype(BF16)
        attn = _nn(vt, probs_b).astype(BF16)
        d_prob = _tn(vt, da)
        delta = jnp.sum(da.astype(F32) * attn.astype(F32), axis=0, keepdims=True)
        d_score = (probs * (d_prob - delta) * scale).astype(BF16)
        dq3[0, lo:lo + HEAD_DIM] = _nn(kt, d_score).astype(BF16)
        dq3[1, lo:lo + HEAD_DIM] = _nt(qt, d_score).astype(BF16)
        dq3[2, lo:lo + HEAD_DIM] = _nt(da, probs_b).astype(BF16)
    dq3[:, W:] = jnp.zeros((3, 256 - W, TOK), BF16)

    f = (f0, f1)
    for t in range(s.T):
        block = xt[t * W:(t + 1) * W]
        for w in range(3):
            g = _nt(block, dq3[w])
            for h in range(2):
                f[h][pl.ds(t * 3 * W + w, W, stride=3)] = g[:, h * 128:(h + 1) * 128]

    def chunk(h, y, z):
        return f[h][pl.ds(pl.multiple_of((y * Z + z) * s.RZ, 8), s.RZ)]

    steps = Z // 2
    ring = {}

    def ring_step(k):
        for d in range(2):
            sign = 1 if d == 0 else -1
            to = at_z((mz + sign + Z) % Z)
            z = (mz + sign * (steps + 1 - k) + Z) % Z
            for h in range(2):
                if k == 1:
                    stage[d, h] = chunk(h, d, z).astype(BF16)
                    copy = send(stage.at[d, h], slots.at[d, h, 0, pl.ds(d * s.RZ, s.RZ)],
                                c_ss.at[d, h, 0], c_rs.at[d, h, 0], to)
                else:
                    ring[d, h, k - 1].wait_recv()
                    for y in range(YH):
                        part = pl.ds(y * s.RZ, s.RZ)
                        own = chunk(h, y, z)
                        if k > 2 or y == d:
                            own = own + slots[d, h, k - 2, part].astype(F32)
                        slots[d, h, k - 2, part] = own.astype(BF16)
                    copy = send(slots.at[d, h, k - 2], slots.at[d, h, k - 1],
                                c_ss.at[d, h, k - 1], c_rs.at[d, h, k - 1], to)
                ring[d, h, k] = copy

    def part(t):
        t = pl.multiple_of(t * W, 16)
        total = _nn(wn[0, pl.ds(t, W)], dq3[0, :W])
        total += _nn(wn[1, pl.ds(t, W)], dq3[1, :W])
        return total + _nn(wn[2, pl.ds(t, W)], dq3[2, :W])

    ring_step(1)
    for l in range(YL):
        ps_s[l] = part(l * C + 1 - mc).astype(BF16)
    pair = send(ps_s, ps_r, pc_ss, pc_rs, at_t(ml, 1 - mc))
    for l in range(YL):
        pown[l] = part(l * C + mc)
    ring_step(2)
    pair.wait_recv()
    for l in range(YL):
        pown[l] = pown[l] + ps_r[l].astype(F32)
        py_s[l] = pown[l].astype(BF16)
    pc = []
    for o in range(1, YL):
        to = (ml + o) % YL
        pc.append(send(py_s.at[to], py_r.at[o - 1], py_ss.at[o - 1], py_rs.at[o - 1], at_t(to, mc)))
    for k in range(3, steps + 1):
        ring_step(k)
    for copy in pc:
        copy.wait_recv()
    total = pown[ml]
    for o in range(1, YL):
        total = total + py_r[o - 1].astype(F32)
    d_out[...] = total.astype(BF16)

    for h in range(2):
        for y in range(YH):
            part_y = pl.ds(y * s.RZ, s.RZ)
            red[h, part_y] = chunk(h, y, mz)
        for d in range(2):
            ring[d, h, steps].wait_recv()
            for y in range(YH):
                part_y = pl.ds(y * s.RZ, s.RZ)
                red[h, part_y] = red[h, part_y] + slots[d, h, steps - 1, part_y].astype(F32)

    def of_x(h, x):
        return jnp.concatenate(
            [red[h, pl.ds(pl.multiple_of(y * s.RZ + x * s.RPD, 8), s.RPD)] for y in range(YH)], axis=0
        )

    xc = []
    for o in range(1, X):
        to = (mx + o) % X
        for h in range(2):
            xs[o - 1, h] = of_x(h, to).astype(BF16)
        xc.append(send(xs.at[o - 1], xr.at[o - 1], x_ss.at[o - 1], x_rs.at[o - 1], at_q(my * X + to)))
    for h in range(2):
        acc[h] = of_x(h, mx)
    for o in range(1, X):
        xc[o - 1].wait_recv()
        for h in range(2):
            acc[h] = acc[h] + xr[o - 1, h].astype(F32)
    other = 1 - my
    yc = send(acc.at[:, pl.ds(pl.multiple_of(other * s.RPD, 8), s.RPD)], yr, y_ss, y_rs, at_q(other * X + mx))
    yc.wait_recv()
    norm = (TOK * s.R) ** (-0.5)
    mine = pl.ds(pl.multiple_of(my * s.RPD, 8), s.RPD)
    g_out[:, :128] = (acc[0, mine] + yr[0]) * norm
    g_out[:, 128:] = ((acc[1, mine] + yr[1]) * norm)[:, :W - 128]

    for copy in zc + qc + sent + list(ring.values()) + [pair] + pc + xc + [yc]:
        copy.wait_send()


def shards(s, loader_rows, pack_dest, segment_ids, w_qkv, w_out, d_out):
    W, TOK, D = s.W, s.TOK, s.D
    Q, Z, X, YL = s.Q, s.Z, s.X, s.YL
    dma = pltpu.SemaphoreType.DMA
    vmem = pl.BlockSpec(memory_space=pltpu.VMEM)
    hbm = pl.BlockSpec(memory_space=pl.ANY)
    steps = Z // 2
    grad, packed = pl.pallas_call(
        functools.partial(_kernel, s),
        out_shape=(
            jax.ShapeDtypeStruct((s.RPD, W), F32),
            jax.ShapeDtypeStruct((W, TOK), BF16),
        ),
        in_specs=[vmem, vmem, vmem, hbm, hbm, vmem, vmem],
        out_specs=(vmem, vmem),
        scratch_shapes=[
            pltpu.VMEM((3 * W, D), BF16),
            pltpu.VMEM((3, D, W), BF16),
            pltpu.VMEM((W, D), BF16),
            pltpu.VMEM((Z * s.B1, 256), BF16),
            pltpu.VMEM((Z * s.B1, 256), BF16),
            pltpu.VMEM((Q * s.B2, 256), BF16),
            pltpu.VMEM((Q * s.B2, 256), BF16),
            pltpu.VMEM((D, TOK), BF16),
            pltpu.VMEM((D, TOK), BF16),
            pltpu.VMEM((3, 256, TOK), BF16),
            pltpu.VMEM((3 * D, 128), F32),
            pltpu.VMEM((3 * D, 128), F32),
            pltpu.VMEM((2, 2, s.RZ, 128), BF16),
            pltpu.VMEM((2, 2, steps, 2 * s.RZ, 128), BF16),
            pltpu.VMEM((2, 2 * s.RZ, 128), F32),
            pltpu.VMEM((X - 1, 2, 2 * s.RPD, 128), BF16),
            pltpu.VMEM((X - 1, 2, 2 * s.RPD, 128), BF16),
            pltpu.VMEM((2, 2 * s.RPD, 128), F32),
            pltpu.VMEM((2, s.RPD, 128), F32),
            pltpu.VMEM((YL, W, TOK), BF16),
            pltpu.VMEM((YL, W, TOK), BF16),
            pltpu.VMEM((YL, W, TOK), F32),
            pltpu.VMEM((YL, W, TOK), BF16),
            pltpu.VMEM((YL - 1, W, TOK), BF16),
            dma((2,)),
            dma((Z - 1,)),
            dma((Z - 1,)),
            dma((Q - 1,)),
            dma((Q - 1,)),
            dma((YL - 1,)),
            dma((YL - 1,)),
            dma((YL,)),
            dma((YL,)),
            dma((YL - 1,)),
            dma((YL - 1,)),
            dma((YL,)),
            dma((YL,)),
            dma((2, 2, steps)),
            dma((2, 2, steps)),
            dma((X - 1,)),
            dma((X - 1,)),
            dma,
            dma,
            dma,
            dma,
            dma((YL - 1,)),
            dma((YL - 1,)),
        ],
        compiler_params=pltpu.CompilerParams(
            collective_id=0, has_side_effects=True, vmem_limit_bytes=50 * 1024 * 1024
        ),
    )(
        loader_rows.T,
        pack_dest.reshape(1, TOK),
        segment_ids,
        jnp.transpose(w_qkv, (1, 2, 0)).reshape(3 * W, D),
        w_out,
        d_out.T,
        jnp.asarray(_regroup(s), BF16),
    )
    return grad, packed.T


def build(mesh, s):
    placed = (
        P("rep", "tp"),
        P("rep"),
        P("rep", None),
        P(None, None, "tp"),
        P("tp", None),
        P("rep", "tp"),
    )
    return jax.shard_map(
        functools.partial(shards, s),
        mesh=mesh,
        in_specs=placed,
        out_specs=(P("rep", "tp"), P("rep", "tp")),
        check_vma=False,
    )


def solution(mesh):
    return build(mesh, Sizes(2, 12, 4, 4, 2, 256, 224))
```

time: 845 us -> 104 us (0.12)
  the two profiles are of different devices: /device:TPU:8 before, /device:TPU:40 now
where the time goes in v1:
time: 104 us; the launch traced here: 103 us
  Pallas kernels  94.6 us (91%)
  local copies, waits for them, and re-layouts  8.2 us (8%)
    pallas_call x1, Pallas kernels, shards(): pl.pallas_call(functools.partial(_kernel, s), out_shape=(jax.ShapeDtypeSt...  94.6 us
    unnamed x16, local copies, waits for them, and re-layouts  8.2 us

profile of v1, /device:TPU:40, one launch (start us, length us, event | category | flops | bytes accessed | tf_op | source)
XLA Modules:
  0.0 103.4 jit_solution(12623321765613675264)
XLA Ops:
  0.6 0.0 copy-start
  0.6 1.7 %copy-done = bf16[1792,3,224]{0,2,1:T(8,128)(2,1)S(1)} copy-done((bf16[1792,3,224]{0,2,1:T(8,128)(2,1)S(1)}, bf16[1792,3,224]{0,2,1:T(8,128)(2,1)}, u32[]{:S(2)}) %copy-start) | copy-done | bytes 2408472
  2.3 0.0 copy-start.1
  2.3 1.1 %copy-done.1 = bf16[224,1792]{1,0:T(8,128)(2,1)S(1)} copy-done((bf16[224,1792]{1,0:T(8,128)(2,1)S(1)}, bf16[224,1792]{1,0:T(8,128)(2,1)}, u32[]{:S(2)}) %copy-start.1) | copy-done | bytes 802840
  3.5 0.0 copy-start.2
  3.5 1.0 copy-done.2
  4.4 0.0 copy-start.3
  4.4 0.9 copy-done.3
  5.3 0.0 copy-start.4
  5.3 0.9 copy-done.4
  6.2 0.0 copy-start.5
  6.2 0.7 copy-done.5
  6.9 0.0 copy-start.6
  6.9 0.7 copy-done.6
  7.6 94.6 %shard_map.86 = (f32[56,224]{1,0:T(8,128)S(1)}, bf16[224,256]{1,0:T(8,128)(2,1)S(1)}) custom-call(bf16[224,256]{1,0:T(8,128)(2,1)S(1)} %bitcast.9, s32[1,256]{1,0:T(1,128)S(1)} %bitcast.11, s32[1,256]{1,0:T(1,128)S(1)} %copy-done.6, bf16[672,1792]{1,0:T(8,128)(2,1)S(1)} %bitcast.7, bf16[224,1792]{1,0:T(8,128)(2,1)S(1)} %copy-done.1, ...), custom_call_target="tpu_custom_call" | custom-call | tf_op jit(solution)/shard_map/pallas_call | solution.py:322
  102.2 0.6 copy.11
  102.8 0.6 copy.12
Async XLA Ops:
  0.6 1.7 %copy-start = (bf16[1792,3,224]{0,2,1:T(8,128)(2,1)S(1)}, bf16[1792,3,224]{0,2,1:T(8,128)(2,1)}, u32[]{:S(2)}) copy-start(bf16[1792,3,224]{0,2,1:T(8,128)(2,1)} %param.10) | copy-start | bytes 7225348
  2.3 1.1 %copy-start.1 = (bf16[224,1792]{1,0:T(8,128)(2,1)S(1)}, bf16[224,1792]{1,0:T(8,128)(2,1)}, u32[]{:S(2)}) copy-start(bf16[224,1792]{1,0:T(8,128)(2,1)} %wo_hbm.1) | copy-start | bytes 2408452
  3.5 1.0 copy-start.2
  4.4 0.9 copy-start.3
  5.3 0.9 copy-start.4
  6.2 0.7 copy-start.5
  6.9 0.7 copy-start.6

commit v2 on v1

--- a/solution.py
+++ b/solution.py
@@ -2,7 +2,6 @@
 
 import jax
 import jax.numpy as jnp
-import numpy as np
 from jax import lax
 from jax.experimental import pallas as pl
 from jax.experimental.pallas import tpu as pltpu
@@ -32,6 +31,18 @@
 
 def _onehot(cond):
     return jnp.where(cond, 1.0, 0.0).astype(BF16)
+
+
+class Copy:
+    def __init__(self, *args, **kw):
+        self.copy = pltpu.make_async_remote_copy(*args, **kw)
+        self.copy.start()
+        self.arrived = False
+
+    def wait_recv(self):
+        if not self.arrived:
+            self.copy.wait_recv()
+            self.arrived = True
 
 
 class Sizes:
@@ -48,23 +59,15 @@
         self.RZ = x * self.RPD
 
 
-def _regroup(s):
-    m = np.zeros((s.Q * s.B2, s.Z * s.B1), np.float32)
-    for q in range(s.Q):
-        for zs in range(s.Z):
-            for j in range(s.CAP):
-                m[q * s.B2 + zs * s.CAP + j, zs * s.B1 + q * s.CAP + j] = 1.0
-    return m
-
-
 def _kernel(
     s,
-    ld, dest, seg, w_hbm, wo_hbm, cot, regroup,
+    ld, dest, seg, w_hbm, wo_hbm, cot,
     g_out, d_out,
-    wv, wn, wo, s1, r1, s2, r2, xt, ct, dq3, f0, f1, stage, slots, red, xs, xr, acc, yr,
+    wv, wn, wo, s1, r1, s2, r2, xt, ct, dq3, f0, f1, a_stage0, a_stage1, a_slots0, a_slots1,
+    b_s, b_r, b_f, b_stage0, b_stage1, b_slots0, b_slots1, red, xs, xr, acc, yr,
     ps_s, ps_r, pown, py_s, py_r,
     w_sem, z_ss, z_rs, q_ss, q_rs, cg_ss, cg_rs, cf_ss, cf_rs, xg_ss, xg_rs, xf_ss, xf_rs,
-    c_ss, c_rs, x_ss, x_rs, y_ss, y_rs, pc_ss, pc_rs, py_ss, py_rs,
+    a_ss, a_rs, b_ss, b_rs, bz_ss, bz_rs, x_ss, x_rs, y_ss, y_rs, pc_ss, pc_rs, py_ss, py_rs,
 ):
     W, TOK, Z, X, YH, YL, C, Q = s.W, s.TOK, s.Z, s.X, s.YH, s.YL, s.C, s.Q
     rep, tp = lax.axis_index("rep"), lax.axis_index("tp")
@@ -87,12 +90,18 @@
         return ref.at[pl.ds(pl.multiple_of(start, unit), size)]
 
     def send(src, dst, ss, rs, device):
-        copy = pltpu.make_async_remote_copy(
+        copy = Copy(
             src_ref=src, dst_ref=dst, send_sem=ss, recv_sem=rs, device_id=device, device_id_type=MESH
         )
-        copy.start()
+        started.append(copy)
         return copy
 
+    def finish():
+        for copy in started:
+            copy.wait_recv()
+            copy.copy.wait_send()
+
+    started = []
     partners = [at_z((mz + o) % Z) for o in range(1, Z)]
     partners += [at_q((mq + o) % Q) for o in range(1, Q)]
     partners += [at_t((ml + o) % YL, mc) for o in range(1, YL)]
@@ -145,7 +154,6 @@
             first[-1].wait_recv()
             for copy in more:
                 copy.wait_recv()
-            return first + more
 
         return rest
 
@@ -157,9 +165,14 @@
         for j in range(0, s.D, 128):
             wn[w, pl.ds(j, 128)] = wv[pl.ds(w * W, W), pl.ds(j, 128)].T
 
+    line = lax.broadcasted_iota(jnp.int32, (1, Z * s.B1), 1)
+    inner = line % s.B1
+    aim = inner // s.CAP * s.B2 + line // s.B1 * s.CAP + inner % s.CAP
+    aim = jnp.where(inner < Q * s.CAP, aim, -1)
+    regroup = _onehot(lax.broadcasted_iota(jnp.int32, (Q * s.B2, Z * s.B1), 0) == aim)
     for copy in zc:
         copy.wait_recv()
-    s2[...] = _nn(regroup[...], r1[...]).astype(BF16)
+    s2[...] = _nn(regroup, r1[...]).astype(BF16)
     qc = []
     for o in range(1, Q):
         to = (mq + o) % Q
@@ -169,7 +182,7 @@
         )
     r2[pl.ds(pl.multiple_of(mq * s.B2, 16), s.B2)] = s2[pl.ds(pl.multiple_of(mq * s.B2, 16), s.B2)]
 
-    sent = cot_rest()
+    cot_rest()
     wo_copy.wait()
     d_attn = _nn(wo[...], ct[...]).astype(BF16)
 
@@ -181,7 +194,7 @@
     put = _onehot(slots_got == iota_s)
     xt[pl.ds(pl.multiple_of(tp * W, 16), W)] = _tn(got, put)[:W].astype(BF16)
     rows_rest = gather(rows(xt, tp * W, W, 16), xt, xg_ss, xg_rs, xf_ss, xf_rs)
-    sent += rows_rest()
+    rows_rest()
 
     qkv = _nn(wv[...], xt[...]).astype(BF16)
     scale = HEAD_DIM ** (-0.5)
@@ -208,6 +221,8 @@
     dq3[:, W:] = jnp.zeros((3, 256 - W, TOK), BF16)
 
     f = (f0, f1)
+    a_stage, a_slots = (a_stage0, a_stage1), (a_slots0, a_slots1)
+    b_stage, b_slots = (b_stage0, b_stage1), (b_slots0, b_slots1)
     for t in range(s.T):
         block = xt[t * W:(t + 1) * W]
         for w in range(3):
@@ -215,33 +230,86 @@
             for h in range(2):
                 f[h][pl.ds(t * 3 * W + w, W, stride=3)] = g[:, h * 128:(h + 1) * 128]
 
-    def chunk(h, y, z):
-        return f[h][pl.ds(pl.multiple_of((y * Z + z) * s.RZ, 8), s.RZ)]
+    def chunk(h, y, z, x, size):
+        return f[h][pl.ds(pl.multiple_of(((y * Z + z) * X + x) * s.RPD, 8), size)]
+
+    def rel(off):
+        return (mz + off + Z) % Z
 
     steps = Z // 2
-    ring = {}
-
-    def ring_step(k):
-        for d in range(2):
-            sign = 1 if d == 0 else -1
-            to = at_z((mz + sign + Z) % Z)
-            z = (mz + sign * (steps + 1 - k) + Z) % Z
-            for h in range(2):
-                if k == 1:
-                    stage[d, h] = chunk(h, d, z).astype(BF16)
-                    copy = send(stage.at[d, h], slots.at[d, h, 0, pl.ds(d * s.RZ, s.RZ)],
-                                c_ss.at[d, h, 0], c_rs.at[d, h, 0], to)
-                else:
-                    ring[d, h, k - 1].wait_recv()
-                    for y in range(YH):
-                        part = pl.ds(y * s.RZ, s.RZ)
-                        own = chunk(h, y, z)
-                        if k > 2 or y == d:
-                            own = own + slots[d, h, k - 2, part].astype(F32)
-                        slots[d, h, k - 2, part] = own.astype(BF16)
-                    copy = send(slots.at[d, h, k - 2], slots.at[d, h, k - 1],
-                                c_ss.at[d, h, k - 1], c_rs.at[d, h, k - 1], to)
-                ring[d, h, k] = copy
+
+    class Ring:
+        def __init__(self, own, stage, slots, ss, rs):
+            self.own, self.stage, self.slots, self.ss, self.rs = own, stage, slots, ss, rs
+            self.copies = {}
+
+        def step(self, k):
+            for i in range(2):
+                for d in range(2):
+                    p = (d + i) % 2
+                    sign = 1 if d == 0 else -1
+                    if k == 1 and p != d:
+                        continue
+                    off = sign * (steps + 1 - k)
+                    term = self.own(p, off)
+                    first = k == (1 if p == d else 2)
+                    if first:
+                        src = self.stage[p].at[d]
+                    else:
+                        self.copies[d, p, k - 1].wait_recv()
+                        src = self.slots[p].at[d, k - 2]
+                        term = term + src[...].astype(F32)
+                    src[...] = term.astype(BF16)
+                    self.copies[d, p, k] = send(
+                        src, self.slots[p].at[d, k - 1], self.ss.at[d, p, k - 1], self.rs.at[d, p, k - 1],
+                        at_z(rel(sign)),
+                    )
+
+        def total(self, p):
+            value = self.own(p, 0)
+            for d in range(2):
+                self.copies[d, p, steps].wait_recv()
+                value = value + self.slots[p][d, steps - 1].astype(F32)
+            return value
+
+    offs = [steps]
+    for k in range(steps - 1, 0, -1):
+        offs += [k, -k]
+    offs += [0]
+    cuts = [0, min(5, len(offs) - 1), len(offs)]
+    two = 2 * s.RPD
+
+    def of_x(h, off, x):
+        return jnp.concatenate([chunk(h, y, rel(off), x, s.RPD) for y in range(YH)], axis=0)
+
+    b_copies = {}
+
+    def b_send(piece):
+        lo, hi = cuts[piece], cuts[piece + 1]
+        for o in range(1, X):
+            to = (mx + o) % X
+            for i in range(lo, hi):
+                b_s[o - 1, i * two:(i + 1) * two] = of_x(1, offs[i], to).astype(BF16)
+            span = pl.ds(lo * two, (hi - lo) * two)
+            b_copies[piece, o] = send(b_s.at[o - 1, span], b_r.at[o - 1, span],
+                                      b_ss.at[o - 1, piece], b_rs.at[o - 1, piece], at_q(my * X + to))
+
+    def b_sum(piece):
+        for o in range(1, X):
+            b_copies[piece, o].wait_recv()
+        for i in range(cuts[piece], cuts[piece + 1]):
+            value = of_x(1, offs[i], mx)
+            for o in range(1, X):
+                value = value + b_r[o - 1, i * two:(i + 1) * two].astype(F32)
+            b_f[i] = value
+
+    half = -(-s.RPD // 16) * 16
+    ends = (0, half, two)
+    ring_a = Ring(lambda p, off: chunk(0, p, rel(off), 0, s.RZ), a_stage, a_slots, a_ss, a_rs)
+    ring_b = Ring(
+        lambda p, off: b_f[offs.index(off) if off in offs else 0, ends[p]:ends[p + 1]],
+        b_stage, b_slots, bz_ss, bz_rs,
+    )
 
     def part(t):
         t = pl.multiple_of(t * W, 16)
@@ -249,13 +317,19 @@
         total += _nn(wn[1, pl.ds(t, W)], dq3[1, :W])
         return total + _nn(wn[2, pl.ds(t, W)], dq3[2, :W])
 
-    ring_step(1)
+    b_send(0)
+    ring_a.step(1)
+    b_send(1)
     for l in range(YL):
         ps_s[l] = part(l * C + 1 - mc).astype(BF16)
     pair = send(ps_s, ps_r, pc_ss, pc_rs, at_t(ml, 1 - mc))
+    ring_a.step(2)
     for l in range(YL):
         pown[l] = part(l * C + mc)
-    ring_step(2)
+    b_sum(0)
+    ring_b.step(1)
+    if steps >= 3:
+        ring_a.step(3)
     pair.wait_recv()
     for l in range(YL):
         pown[l] = pown[l] + ps_r[l].astype(F32)
@@ -264,8 +338,27 @@
     for o in range(1, YL):
         to = (ml + o) % YL
         pc.append(send(py_s.at[to], py_r.at[o - 1], py_ss.at[o - 1], py_rs.at[o - 1], at_t(to, mc)))
-    for k in range(3, steps + 1):
-        ring_step(k)
+    ring_b.step(2)
+    b_sum(1)
+    for k in range(4, steps + 1):
+        ring_a.step(k)
+        ring_b.step(k - 1)
+    for k in range(max(3, steps), steps + 1):
+        ring_b.step(k)
+    for y in range(YH):
+        red[y * s.RZ:(y + 1) * s.RZ] = ring_a.total(y)
+
+    def red_x(x):
+        return jnp.concatenate(
+            [red[pl.ds(pl.multiple_of(y * s.RZ + x * s.RPD, 8), s.RPD)] for y in range(YH)], axis=0
+        )
+
+    xc = []
+    for o in range(1, X):
+        to = (mx + o) % X
+        xs[o - 1] = red_x(to).astype(BF16)
+        xc.append(send(xs.at[o - 1], xr.at[o - 1], x_ss.at[o - 1], x_rs.at[o - 1], at_q(my * X + to)))
+
     for copy in pc:
         copy.wait_recv()
     total = pown[ml]
@@ -273,33 +366,14 @@
         total = total + py_r[o - 1].astype(F32)
     d_out[...] = total.astype(BF16)
 
-    for h in range(2):
-        for y in range(YH):
-            part_y = pl.ds(y * s.RZ, s.RZ)
-            red[h, part_y] = chunk(h, y, mz)
-        for d in range(2):
-            ring[d, h, steps].wait_recv()
-            for y in range(YH):
-                part_y = pl.ds(y * s.RZ, s.RZ)
-                red[h, part_y] = red[h, part_y] + slots[d, h, steps - 1, part_y].astype(F32)
-
-    def of_x(h, x):
-        return jnp.concatenate(
-            [red[h, pl.ds(pl.multiple_of(y * s.RZ + x * s.RPD, 8), s.RPD)] for y in range(YH)], axis=0
-        )
-
-    xc = []
-    for o in range(1, X):
-        to = (mx + o) % X
-        for h in range(2):
-            xs[o - 1, h] = of_x(h, to).astype(BF16)
-        xc.append(send(xs.at[o - 1], xr.at[o - 1], x_ss.at[o - 1], x_rs.at[o - 1], at_q(my * X + to)))
-    for h in range(2):
-        acc[h] = of_x(h, mx)
+    for p in range(2):
+        acc[1, ends[p]:ends[p + 1]] = ring_b.total(p)
+    value = red_x(mx)
     for o in range(1, X):
         xc[o - 1].wait_recv()
-        for h in range(2):
-            acc[h] = acc[h] + xr[o - 1, h].astype(F32)
+        value = value + xr[o - 1].astype(F32)
+    acc[0] = value
+
     other = 1 - my
     yc = send(acc.at[:, pl.ds(pl.multiple_of(other * s.RPD, 8), s.RPD)], yr, y_ss, y_rs, at_q(other * X + mx))
     yc.wait_recv()
@@ -308,8 +382,7 @@
     g_out[:, :128] = (acc[0, mine] + yr[0]) * norm
     g_out[:, 128:] = ((acc[1, mine] + yr[1]) * norm)[:, :W - 128]
 
-    for copy in zc + qc + sent + list(ring.values()) + [pair] + pc + xc + [yc]:
-        copy.wait_send()
+    finish()
 
 
 def shards(s, loader_rows, pack_dest, segment_ids, w_qkv, w_out, d_out):
@@ -319,13 +392,14 @@
     vmem = pl.BlockSpec(memory_space=pltpu.VMEM)
     hbm = pl.BlockSpec(memory_space=pl.ANY)
     steps = Z // 2
+    two, half = 2 * s.RPD, -(-s.RPD // 16) * 16
     grad, packed = pl.pallas_call(
         functools.partial(_kernel, s),
         out_shape=(
             jax.ShapeDtypeStruct((s.RPD, W), F32),
             jax.ShapeDtypeStruct((W, TOK), BF16),
         ),
-        in_specs=[vmem, vmem, vmem, hbm, hbm, vmem, vmem],
+        in_specs=[vmem, vmem, vmem, hbm, hbm, vmem],
         out_specs=(vmem, vmem),
         scratch_shapes=[
             pltpu.VMEM((3 * W, D), BF16),
@@ -340,11 +414,20 @@
             pltpu.VMEM((3, 256, TOK), BF16),
             pltpu.VMEM((3 * D, 128), F32),
             pltpu.VMEM((3 * D, 128), F32),
-            pltpu.VMEM((2, 2, s.RZ, 128), BF16),
-            pltpu.VMEM((2, 2, steps, 2 * s.RZ, 128), BF16),
-            pltpu.VMEM((2, 2 * s.RZ, 128), F32),
-            pltpu.VMEM((X - 1, 2, 2 * s.RPD, 128), BF16),
-            pltpu.VMEM((X - 1, 2, 2 * s.RPD, 128), BF16),
+            pltpu.VMEM((2, s.RZ, 128), BF16),
+            pltpu.VMEM((2, s.RZ, 128), BF16),
+            pltpu.VMEM((2, steps, s.RZ, 128), BF16),
+            pltpu.VMEM((2, steps, s.RZ, 128), BF16),
+            pltpu.VMEM((X - 1, Z * two, 128), BF16),
+            pltpu.VMEM((X - 1, Z * two, 128), BF16),
+            pltpu.VMEM((Z, two, 128), F32),
+            pltpu.VMEM((2, half, 128), BF16),
+            pltpu.VMEM((2, two - half, 128), BF16),
+            pltpu.VMEM((2, steps, half, 128), BF16),
+            pltpu.VMEM((2, steps, two - half, 128), BF16),
+            pltpu.VMEM((2 * s.RZ, 128), F32),
+            pltpu.VMEM((X - 1, two, 128), BF16),
+            pltpu.VMEM((X - 1, two, 128), BF16),
             pltpu.VMEM((2, 2 * s.RPD, 128), F32),
             pltpu.VMEM((2, s.RPD, 128), F32),
             pltpu.VMEM((YL, W, TOK), BF16),
@@ -367,6 +450,10 @@
             dma((YL,)),
             dma((2, 2, steps)),
             dma((2, 2, steps)),
+            dma((X - 1, 2)),
+            dma((X - 1, 2)),
+            dma((2, 2, steps)),
+            dma((2, 2, steps)),
             dma((X - 1,)),
             dma((X - 1,)),
             dma,
@@ -377,7 +464,7 @@
             dma((YL - 1,)),
         ],
         compiler_params=pltpu.CompilerParams(
-            collective_id=0, has_side_effects=True, vmem_limit_bytes=50 * 1024 * 1024
+            collective_id=0, has_side_effects=True, vmem_limit_bytes=60 * 1024 * 1024
         ),
     )(
         loader_rows.T,
@@ -386,7 +473,6 @@
         jnp.transpose(w_qkv, (1, 2, 0)).reshape(3 * W, D),
         w_out,
         d_out.T,
-        jnp.asarray(_regroup(s), BF16),
     )
     return grad, packed.T
 

time: 104 us -> 98.7 us (0.949)
  the two profiles are of different devices: /device:TPU:40 before, /device:TPU:24 now
where the time goes in v2:
time: 98.7 us; the launch traced here: 98.5 us
  Pallas kernels  94.8 us (96%)
  local copies, waits for them, and re-layouts  3 us (3%)
    pallas_call x1, Pallas kernels, shards(): pl.pallas_call(functools.partial(_kernel, s), out_shape=(jax.ShapeDtypeSt...  94.8 us
    unnamed x2, local copies, waits for them, and re-layouts  3 us

profile of v2, /device:TPU:24, one launch (start us, length us, event | category | flops | bytes accessed | tf_op | source)
XLA Modules:
  0.0 98.5 jit_solution(8265694879050911166)
XLA Ops:
  0.6 94.8 %shard_map.77 = (f32[56,224]{1,0:T(8,128)}, bf16[224,256]{1,0:T(8,128)(2,1)}) custom-call(bf16[224,256]{1,0:T(8,128)(2,1)} %bitcast.9, s32[1,256]{1,0:T(1,128)} %bitcast.11, s32[1,256]{1,0:T(1,128)} %seg.1, bf16[672,1792]{1,0:T(8,128)(2,1)} %bitcast.7, bf16[224,1792]{1,0:T(8,128)(2,1)} %wo_hbm.1, bf16[224,256]{1,0:T(8,128)(2,1)} %bitcast.10), custom_call_target="tpu_custom_call" | custom-call | tf_op jit(solution)/shard_map/pallas_call | solution.py:396
  95.5 1.4 %copy.10 = f32[56,224]{1,0:T(8,128)} copy(f32[56,224]{1,0:T(8,128)} %get-tuple-element.8) | data formatting | bytes 100352
  96.9 1.6 %copy.11 = bf16[256,224]{0,1:T(8,128)(2,1)} copy(bf16[256,224]{0,1:T(8,128)(2,1)} %bitcast.8) | data formatting | bytes 229376

commit v3 on v2

--- a/solution.py
+++ b/solution.py
@@ -8,6 +8,7 @@
 from jax.sharding import PartitionSpec as P
 
 HEAD_DIM = 112
+A_PARTS = 4
 MESH = pl.DeviceIdType.MESH
 F32 = jnp.float32
 BF16 = jnp.bfloat16
@@ -63,8 +64,8 @@
     s,
     ld, dest, seg, w_hbm, wo_hbm, cot,
     g_out, d_out,
-    wv, wn, wo, s1, r1, s2, r2, xt, ct, dq3, f0, f1, a_stage0, a_stage1, a_slots0, a_slots1,
-    b_s, b_r, b_f, b_stage0, b_stage1, b_slots0, b_slots1, red, xs, xr, acc, yr,
+    wv, wn, wo, s1, r1, s2, r2, xt, ct, dq3, f0, f1, a_stage, a_slots,
+    b_s, b_r, b_f, b_stage, b_slots, red, xs, xr, acc, yr,
     ps_s, ps_r, pown, py_s, py_r,
     w_sem, z_ss, z_rs, q_ss, q_rs, cg_ss, cg_rs, cf_ss, cf_rs, xg_ss, xg_rs, xf_ss, xf_rs,
     a_ss, a_rs, b_ss, b_rs, bz_ss, bz_rs, x_ss, x_rs, y_ss, y_rs, pc_ss, pc_rs, py_ss, py_rs,
@@ -221,8 +222,6 @@
     dq3[:, W:] = jnp.zeros((3, 256 - W, TOK), BF16)
 
     f = (f0, f1)
-    a_stage, a_slots = (a_stage0, a_stage1), (a_slots0, a_slots1)
-    b_stage, b_slots = (b_stage0, b_stage1), (b_slots0, b_slots1)
     for t in range(s.T):
         block = xt[t * W:(t + 1) * W]
         for w in range(3):
@@ -238,45 +237,49 @@
 
     steps = Z // 2
 
-    class Ring:
-        def __init__(self, own, stage, slots, ss, rs):
-            self.own, self.stage, self.slots, self.ss, self.rs = own, stage, slots, ss, rs
-            self.copies = {}
-
-        def step(self, k):
-            for i in range(2):
-                for d in range(2):
-                    p = (d + i) % 2
-                    sign = 1 if d == 0 else -1
-                    if k == 1 and p != d:
-                        continue
-                    off = sign * (steps + 1 - k)
-                    term = self.own(p, off)
-                    first = k == (1 if p == d else 2)
-                    if first:
-                        src = self.stage[p].at[d]
-                    else:
-                        self.copies[d, p, k - 1].wait_recv()
-                        src = self.slots[p].at[d, k - 2]
-                        term = term + src[...].astype(F32)
-                    src[...] = term.astype(BF16)
-                    self.copies[d, p, k] = send(
-                        src, self.slots[p].at[d, k - 1], self.ss.at[d, p, k - 1], self.rs.at[d, p, k - 1],
-                        at_z(rel(sign)),
-                    )
-
-        def total(self, p):
-            value = self.own(p, 0)
+    a_len = YH * s.RZ // A_PARTS
+
+    def a_own(p, off):
+        per_y = A_PARTS // YH
+        start = (p // per_y * Z + rel(off)) * s.RZ + p % per_y * a_len
+        return f0[pl.ds(pl.multiple_of(start, 8), a_len)]
+
+    a_copies = {}
+
+    def a_step(k):
+        for i in range(A_PARTS):
             for d in range(2):
-                self.copies[d, p, steps].wait_recv()
-                value = value + self.slots[p][d, steps - 1].astype(F32)
-            return value
+                p = (i + d * A_PARTS // 2) % A_PARTS
+                owner = p * 2 // A_PARTS
+                if k == 1 and owner != d:
+                    continue
+                sign = 1 if d == 0 else -1
+                term = a_own(p, sign * (steps + 1 - k))
+                if k == (1 if owner == d else 2):
+                    src = a_stage.at[p, d]
+                else:
+                    a_copies[d, p, k - 1].wait_recv()
+                    src = a_slots.at[d, p, k - 2]
+                    term = term + src[...].astype(F32)
+                src[...] = term.astype(BF16)
+                a_copies[d, p, k] = send(
+                    src, a_slots.at[d, p, k - 1], a_ss.at[d, p, k - 1], a_rs.at[d, p, k - 1], at_z(rel(sign))
+                )
+
+    def a_total(p):
+        value = a_own(p, 0)
+        for d in range(2):
+            a_copies[d, p, steps].wait_recv()
+            value = value + a_slots[d, p, steps - 1].astype(F32)
+        return value
 
     offs = [steps]
+    cuts = [0, 1]
     for k in range(steps - 1, 0, -1):
         offs += [k, -k]
+        cuts += [len(offs)]
     offs += [0]
-    cuts = [0, min(5, len(offs) - 1), len(offs)]
+    cuts += [len(offs)]
     two = 2 * s.RPD
 
     def of_x(h, off, x):
@@ -305,11 +308,26 @@
 
     half = -(-s.RPD // 16) * 16
     ends = (0, half, two)
-    ring_a = Ring(lambda p, off: chunk(0, p, rel(off), 0, s.RZ), a_stage, a_slots, a_ss, a_rs)
-    ring_b = Ring(
-        lambda p, off: b_f[offs.index(off) if off in offs else 0, ends[p]:ends[p + 1]],
-        b_stage, b_slots, bz_ss, bz_rs,
-    )
+    b_ring = {}
+
+    def b_step(k):
+        b_sum(k - 1)
+        for d in range(2):
+            sign = 1 if d == 0 else -1
+            i = offs.index(sign * (steps + 1 - k)) if k > 1 else 0
+            span = pl.ds(ends[d], ends[d + 1] - ends[d])
+            if k == 1:
+                b_stage[span] = b_f[i, span].astype(BF16)
+                src, dst = b_stage.at[span], b_slots.at[d, 0, span]
+            else:
+                b_ring[d, k - 1].wait_recv()
+                if k == 2:
+                    b_f[i, span] = b_f[i, span] + b_slots[d, 0, span].astype(F32)
+                    b_slots[d, 0] = b_f[i].astype(BF16)
+                else:
+                    b_slots[d, k - 2] = (b_f[i] + b_slots[d, k - 2].astype(F32)).astype(BF16)
+                src, dst = b_slots.at[d, k - 2], b_slots.at[d, k - 1]
+            b_ring[d, k] = send(src, dst, bz_ss.at[d, k - 1], bz_rs.at[d, k - 1], at_z(rel(sign)))
 
     def part(t):
         t = pl.multiple_of(t * W, 16)
@@ -317,19 +335,18 @@
         total += _nn(wn[1, pl.ds(t, W)], dq3[1, :W])
         return total + _nn(wn[2, pl.ds(t, W)], dq3[2, :W])
 
-    b_send(0)
-    ring_a.step(1)
-    b_send(1)
+    for piece in range(2):
+        b_send(piece)
+    a_step(1)
+    for piece in range(2, len(cuts) - 1):
+        b_send(piece)
     for l in range(YL):
         ps_s[l] = part(l * C + 1 - mc).astype(BF16)
     pair = send(ps_s, ps_r, pc_ss, pc_rs, at_t(ml, 1 - mc))
-    ring_a.step(2)
+    b_step(1)
+    a_step(2)
     for l in range(YL):
         pown[l] = part(l * C + mc)
-    b_sum(0)
-    ring_b.step(1)
-    if steps >= 3:
-        ring_a.step(3)
     pair.wait_recv()
     for l in range(YL):
         pown[l] = pown[l] + ps_r[l].astype(F32)
@@ -338,26 +355,31 @@
     for o in range(1, YL):
         to = (ml + o) % YL
         pc.append(send(py_s.at[to], py_r.at[o - 1], py_ss.at[o - 1], py_rs.at[o - 1], at_t(to, mc)))
-    ring_b.step(2)
-    b_sum(1)
-    for k in range(4, steps + 1):
-        ring_a.step(k)
-        ring_b.step(k - 1)
-    for k in range(max(3, steps), steps + 1):
-        ring_b.step(k)
-    for y in range(YH):
-        red[y * s.RZ:(y + 1) * s.RZ] = ring_a.total(y)
-
-    def red_x(x):
-        return jnp.concatenate(
-            [red[pl.ds(pl.multiple_of(y * s.RZ + x * s.RPD, 8), s.RPD)] for y in range(YH)], axis=0
-        )
-
+    for k in range(2, steps + 1):
+        b_step(k)
+        if k < steps:
+            a_step(k + 1)
+    b_sum(steps)
+    value = b_f[len(offs) - 1]
+    for d in range(2):
+        b_ring[d, steps].wait_recv()
+        value = value + b_slots[d, steps - 1].astype(F32)
+    acc[...] = value
+    other = 1 - my
+    yc = send(acc.at[pl.ds(pl.multiple_of(other * s.RPD, 8), s.RPD)], yr, y_ss, y_rs, at_q(other * X + mx))
+
+    for p in range(A_PARTS):
+        red[p * a_len:(p + 1) * a_len] = a_total(p)
+
+    def red_q(q):
+        return red[pl.ds(pl.multiple_of(q * s.RPD, 8), s.RPD)]
+
+    fill = jnp.zeros((xs.shape[1] - s.RPD, 128), F32)
     xc = []
-    for o in range(1, X):
-        to = (mx + o) % X
-        xs[o - 1] = red_x(to).astype(BF16)
-        xc.append(send(xs.at[o - 1], xr.at[o - 1], x_ss.at[o - 1], x_rs.at[o - 1], at_q(my * X + to)))
+    for o in range(1, Q):
+        to = (mq + o) % Q
+        xs[o - 1] = jnp.concatenate([red_q(to), fill], axis=0).astype(BF16)
+        xc.append(send(xs.at[o - 1], xr.at[o - 1], x_ss.at[o - 1], x_rs.at[o - 1], at_q(to)))
 
     for copy in pc:
         copy.wait_recv()
@@ -366,21 +388,15 @@
         total = total + py_r[o - 1].astype(F32)
     d_out[...] = total.astype(BF16)
 
-    for p in range(2):
-        acc[1, ends[p]:ends[p + 1]] = ring_b.total(p)
-    value = red_x(mx)
-    for o in range(1, X):
+    value = red_q(mq)
+    for o in range(1, Q):
         xc[o - 1].wait_recv()
-        value = value + xr[o - 1].astype(F32)
-    acc[0] = value
-
-    other = 1 - my
-    yc = send(acc.at[:, pl.ds(pl.multiple_of(other * s.RPD, 8), s.RPD)], yr, y_ss, y_rs, at_q(other * X + mx))
+        value = value + xr[o - 1, :s.RPD].astype(F32)
     yc.wait_recv()
     norm = (TOK * s.R) ** (-0.5)
     mine = pl.ds(pl.multiple_of(my * s.RPD, 8), s.RPD)
-    g_out[:, :128] = (acc[0, mine] + yr[0]) * norm
-    g_out[:, 128:] = ((acc[1, mine] + yr[1]) * norm)[:, :W - 128]
+    g_out[:, :128] = value * norm
+    g_out[:, 128:] = ((acc[mine] + yr[...]) * norm)[:, :W - 128]
 
     finish()
 
@@ -392,7 +408,7 @@
     vmem = pl.BlockSpec(memory_space=pltpu.VMEM)
     hbm = pl.BlockSpec(memory_space=pl.ANY)
     steps = Z // 2
-    two, half = 2 * s.RPD, -(-s.RPD // 16) * 16
+    two = 2 * s.RPD
     grad, packed = pl.pallas_call(
         functools.partial(_kernel, s),
         out_shape=(
@@ -414,22 +430,18 @@
             pltpu.VMEM((3, 256, TOK), BF16),
             pltpu.VMEM((3 * D, 128), F32),
             pltpu.VMEM((3 * D, 128), F32),
-            pltpu.VMEM((2, s.RZ, 128), BF16),
-            pltpu.VMEM((2, s.RZ, 128), BF16),
-            pltpu.VMEM((2, steps, s.RZ, 128), BF16),
-            pltpu.VMEM((2, steps, s.RZ, 128), BF16),
+            pltpu.VMEM((A_PARTS, 2, 2 * s.RZ // A_PARTS, 128), BF16),
+            pltpu.VMEM((2, A_PARTS, steps, 2 * s.RZ // A_PARTS, 128), BF16),
             pltpu.VMEM((X - 1, Z * two, 128), BF16),
             pltpu.VMEM((X - 1, Z * two, 128), BF16),
             pltpu.VMEM((Z, two, 128), F32),
-            pltpu.VMEM((2, half, 128), BF16),
-            pltpu.VMEM((2, two - half, 128), BF16),
-            pltpu.VMEM((2, steps, half, 128), BF16),
-            pltpu.VMEM((2, steps, two - half, 128), BF16),
+            pltpu.VMEM((two, 128), BF16),
+            pltpu.VMEM((2, steps, two, 128), BF16),
             pltpu.VMEM((2 * s.RZ, 128), F32),
-            pltpu.VMEM((X - 1, two, 128), BF16),
-            pltpu.VMEM((X - 1, two, 128), BF16),
-            pltpu.VMEM((2, 2 * s.RPD, 128), F32),
-            pltpu.VMEM((2, s.RPD, 128), F32),
+            pltpu.VMEM((Q - 1, -(-s.RPD // 16) * 16, 128), BF16),
+            pltpu.VMEM((Q - 1, -(-s.RPD // 16) * 16, 128), BF16),
+            pltpu.VMEM((2 * s.RPD, 128), F32),
+            pltpu.VMEM((s.RPD, 128), F32),
             pltpu.VMEM((YL, W, TOK), BF16),
             pltpu.VMEM((YL, W, TOK), BF16),
             pltpu.VMEM((YL, W, TOK), F32),
@@ -440,22 +452,22 @@
             dma((Z - 1,)),
             dma((Q - 1,)),
             dma((Q - 1,)),
-            dma((YL - 1,)),
-            dma((YL - 1,)),
-            dma((YL,)),
-            dma((YL,)),
-            dma((YL - 1,)),
-            dma((YL - 1,)),
-            dma((YL,)),
-            dma((YL,)),
-            dma((2, 2, steps)),
-            dma((2, 2, steps)),
-            dma((X - 1, 2)),
-            dma((X - 1, 2)),
-            dma((2, 2, steps)),
-            dma((2, 2, steps)),
-            dma((X - 1,)),
-            dma((X - 1,)),
+            dma((YL,)),
+            dma((YL,)),
+            dma((YL,)),
+            dma((YL,)),
+            dma((YL,)),
+            dma((YL,)),
+            dma((YL,)),
+            dma((YL,)),
+            dma((2, A_PARTS, steps)),
+            dma((2, A_PARTS, steps)),
+            dma((X - 1, steps + 1)),
+            dma((X - 1, steps + 1)),
+            dma((2, steps)),
+            dma((2, steps)),
+            dma((Q - 1,)),
+            dma((Q - 1,)),
             dma,
             dma,
             dma,

time: 98.7 us -> 89.7 us (0.909)
  the two profiles are of different devices: /device:TPU:24 before, /device:TPU:30 now
where the time goes in v3:
time: 89.7 us; the launch traced here: 89.5 us
  Pallas kernels  85.9 us (96%)
  local copies, waits for them, and re-layouts  3 us (3%)
    pallas_call x1, Pallas kernels, shards(): pl.pallas_call(functools.partial(_kernel, s), out_shape=(jax.ShapeDtypeSt...  85.9 us
    unnamed x2, local copies, waits for them, and re-layouts  3 us

profile of v3, /device:TPU:30, one launch (start us, length us, event | category | flops | bytes accessed | tf_op | source)
XLA Modules:
  0.0 89.5 jit_solution(6393662964609887527)
XLA Ops:
  0.6 85.9 %shard_map.77 = (f32[56,224]{1,0:T(8,128)}, bf16[224,256]{1,0:T(8,128)(2,1)}) custom-call(bf16[224,256]{1,0:T(8,128)(2,1)} %bitcast.9, s32[1,256]{1,0:T(1,128)} %bitcast.11, s32[1,256]{1,0:T(1,128)} %seg.1, bf16[672,1792]{1,0:T(8,128)(2,1)} %bitcast.7, bf16[224,1792]{1,0:T(8,128)(2,1)} %wo_hbm.1, bf16[224,256]{1,0:T(8,128)(2,1)} %bitcast.10), custom_call_target="tpu_custom_call" | custom-call | tf_op jit(solution)/shard_map/pallas_call | solution.py:412
  86.5 1.4 %copy.10 = f32[56,224]{1,0:T(8,128)} copy(f32[56,224]{1,0:T(8,128)} %get-tuple-element.8) | data formatting | bytes 100352
  87.9 1.6 %copy.11 = bf16[256,224]{0,1:T(8,128)(2,1)} copy(bf16[256,224]{0,1:T(8,128)(2,1)} %bitcast.8) | data formatting | bytes 229376

commit v4 on v3

--- a/solution.py
+++ b/solution.py
@@ -39,11 +39,17 @@
         self.copy = pltpu.make_async_remote_copy(*args, **kw)
         self.copy.start()
         self.arrived = False
+        self.left = False
 
     def wait_recv(self):
         if not self.arrived:
             self.copy.wait_recv()
             self.arrived = True
+
+    def wait_send(self):
+        if not self.left:
+            self.copy.wait_send()
+            self.left = True
 
 
 class Sizes:
@@ -97,14 +103,25 @@
         started.append(copy)
         return copy
 
+    def settle():
+        for copy in started:
+            if copy.arrived:
+                copy.wait_send()
+
     def finish():
         for copy in started:
             copy.wait_recv()
-            copy.copy.wait_send()
+            copy.wait_send()
+
+    others = [(dy, dx) for dy in range(YH - 1, -1, -1) for dx in range(X) if dy or dx]
+
+    def q_of(o):
+        dy, dx = others[o - 1]
+        return (my + dy) % YH * X + (mx + dx) % X
 
     started = []
     partners = [at_z((mz + o) % Z) for o in range(1, Z)]
-    partners += [at_q((mq + o) % Q) for o in range(1, Q)]
+    partners += [at_q(q_of(o)) for o in range(1, Q)]
     partners += [at_t((ml + o) % YL, mc) for o in range(1, YL)]
     partners += [at_t(ml, 1 - mc)]
     barrier = pltpu.get_barrier_semaphore()
@@ -133,7 +150,7 @@
     pl.semaphore_wait(barrier, len(partners))
 
     zc = []
-    for o in range(1, Z):
+    for o in sorted(range(1, Z), key=lambda o: -min(o, Z - o)):
         to = (mz + o) % Z
         zc.append(
             send(rows(s1, to * s.B1, s.B1, 16), rows(r1, mz * s.B1, s.B1, 16),
@@ -143,16 +160,16 @@
 
     def gather(src, buf, ss, rs, fs, fr):
         mine = rows(buf, tp * W, W, 16)
-        first = [send(src, mine, ss.at[o - 1], rs.at[o - 1], at_t((ml + o) % YL, mc)) for o in range(1, YL)]
-        first.append(send(src, mine, fs.at[0], fr.at[0], at_t(ml, 1 - mc)))
+        first = [send(src, mine, fs.at[0], fr.at[0], at_t(ml, 1 - mc))]
+        first += [send(src, mine, ss.at[o - 1], rs.at[o - 1], at_t((ml + o) % YL, mc)) for o in range(1, YL)]
 
         def rest():
             more = []
             for o in range(1, YL):
-                first[o - 1].wait_recv()
+                first[o].wait_recv()
                 there = rows(buf, ((ml - o + YL) % YL * C + mc) * W, W, 16)
                 more.append(send(there, there, fs.at[o], fr.at[o], at_t(ml, 1 - mc)))
-            first[-1].wait_recv()
+            first[0].wait_recv()
             for copy in more:
                 copy.wait_recv()
 
@@ -176,7 +193,7 @@
     s2[...] = _nn(regroup, r1[...]).astype(BF16)
     qc = []
     for o in range(1, Q):
-        to = (mq + o) % Q
+        to = q_of(o)
         qc.append(
             send(rows(s2, to * s.B2, s.B2, 16), rows(r2, mq * s.B2, s.B2, 16),
                  q_ss.at[o - 1], q_rs.at[o - 1], at_q(to))
@@ -340,6 +357,7 @@
     a_step(1)
     for piece in range(2, len(cuts) - 1):
         b_send(piece)
+    settle()
     for l in range(YL):
         ps_s[l] = part(l * C + 1 - mc).astype(BF16)
     pair = send(ps_s, ps_r, pc_ss, pc_rs, at_t(ml, 1 - mc))
@@ -377,9 +395,10 @@
     fill = jnp.zeros((xs.shape[1] - s.RPD, 128), F32)
     xc = []
     for o in range(1, Q):
-        to = (mq + o) % Q
+        to = q_of(o)
         xs[o - 1] = jnp.concatenate([red_q(to), fill], axis=0).astype(BF16)
         xc.append(send(xs.at[o - 1], xr.at[o - 1], x_ss.at[o - 1], x_rs.at[o - 1], at_q(to)))
+    settle()
 
     for copy in pc:
         copy.wait_recv()

time: 89.7 us -> 90.2 us (level)
  the two profiles are of different devices: /device:TPU:30 before, /device:TPU:8 now
where the time goes in v4:
time: 90.2 us; the launch traced here: 89.9 us
  Pallas kernels  86.3 us (96%)
  local copies, waits for them, and re-layouts  3 us (3%)
    pallas_call x1, Pallas kernels, shards(): pl.pallas_call(functools.partial(_kernel, s), out_shape=(jax.ShapeDtypeSt...  86.3 us
    unnamed x2, local copies, waits for them, and re-layouts  3 us

profile of v4, /device:TPU:8, one launch (start us, length us, event | category | flops | bytes accessed | tf_op | source)
XLA Modules:
  0.0 89.9 jit_solution(12801840282856325189)
XLA Ops:
  0.6 86.3 %shard_map.77 = (f32[56,224]{1,0:T(8,128)}, bf16[224,256]{1,0:T(8,128)(2,1)}) custom-call(bf16[224,256]{1,0:T(8,128)(2,1)} %bitcast.9, s32[1,256]{1,0:T(1,128)} %bitcast.11, s32[1,256]{1,0:T(1,128)} %seg.1, bf16[672,1792]{1,0:T(8,128)(2,1)} %bitcast.7, bf16[224,1792]{1,0:T(8,128)(2,1)} %wo_hbm.1, bf16[224,256]{1,0:T(8,128)(2,1)} %bitcast.10), custom_call_target="tpu_custom_call" | custom-call | tf_op jit(solution)/shard_map/pallas_call | solution.py:431
  86.9 1.4 %copy.10 = f32[56,224]{1,0:T(8,128)} copy(f32[56,224]{1,0:T(8,128)} %get-tuple-element.8) | data formatting | bytes 100352
  88.4 1.6 %copy.11 = bf16[256,224]{0,1:T(8,128)(2,1)} copy(bf16[256,224]{0,1:T(8,128)(2,1)} %bitcast.8) | data formatting | bytes 229376
